TPU v7x, 32 devices: a whole 2x2x4 slice. The times are simulated.
32 devices in a mesh: dp: 4 (over x, core), seq: 8 (over z, y).
Axes of the slice: x: 2, y: 2, z: 4, core: 2. Of those that a mesh axis runs over, the one named last changes fastest.
Arguments:
- ssm_input: bfloat16 [4, 2048, 1024], P('dp', 'seq'), may hold values from -6 to 6
- gate_input: bfloat16 [4, 2048, 1024], P('dp', 'seq'), may hold values from -6 to 6
- state_proj: bfloat16 [4, 2048, 512], P('dp', 'seq'), may hold values from -6 to 6
- step_raw: float32 [4, 32, 2048], P('dp', None, 'seq'), may hold values from -5 to 400
- decay_log: float32 [2, 16], replicated, may hold values from -10 to 0
- skip_gain: float32 [16], replicated, may hold values from 0.5 to 2
- norm_gain: float32 [1024], replicated, may hold values from 0.25 to 1.75
- out_weight: bfloat16 [1024, 1024], P('dp'), may hold values from -0.1875 to 0.1875
- latents: bfloat16 [256, 1024], replicated, may hold values from -450 to 450
- lengths: int32 [4], P('dp'), may hold values from 1024 to 2048, as said below
Outputs:
- encoded: bfloat16 [4, 2048, 1024], P('dp', 'seq')
- pooled: bfloat16 [4, 256, 1024], P('dp')
Inputs may be any that keep to these rules, and one draw needn't show every extreme that they name: `lengths`: positions at or after a sequence's length are padding; at least one sequence has none, and one has 1024 real tokens.
All inputs are finite; a program needn't handle non-finite values.
Results may differ from a plain program's by a relative error of at most 0.034.
Values may be sent and summed in bfloat16 or wider, within the bound.
A program may use at most 128 MiB of HBM per device.

v0:
```python
import math

import jax
import jax.numpy as jnp
from jax import lax
from jax.sharding import PartitionSpec as P

BLOCK = 128


def carried_in(part, axis, combine, identity, reverse):
    count = lax.axis_size(axis)
    place = lax.axis_index(axis)
    ahead = count - 1 - place if reverse else place
    gathered = jax.tree.map(lambda a: lax.all_gather(a, axis), part)
    state = jax.tree.map(lambda a, e: jnp.zeros_like(a) + jnp.asarray(e, a.dtype), part, identity)

    def one(hop, state):
        source = count - 1 - hop if reverse else hop
        return combine(
            state, jax.tree.map(lambda a: lax.dynamic_index_in_dim(a, source, 0, False), gathered)
        )

    return lax.fori_loop(0, ahead, one, state)


def block_terms(x_block, dt_block, b_block, c_block, forget_rate):
    cumulative = jnp.cumsum(-dt_block * forget_rate[:, None], axis=1)
    gram_matrix = jnp.einsum("qn,kn->qk", c_block, b_block, preferred_element_type=jnp.float32)
    symbol_offset = jnp.arange(x_block.shape[0], dtype=jnp.int32)
    causal = symbol_offset[:, None] >= symbol_offset[None, :]
    spread = jnp.where(causal[None], cumulative[:, :, None] - cumulative[:, None, :], -jnp.inf)
    mixing = (gram_matrix[None] * jnp.exp(spread) * dt_block[:, None, :]).astype(jnp.bfloat16)
    intra_out = jnp.einsum("hqk,khp->qhp", mixing, x_block, preferred_element_type=jnp.float32)
    tail_weight = jnp.exp(cumulative[:, -1:] - cumulative) * dt_block
    scaled_x = (x_block * tail_weight.T[:, :, None]).astype(jnp.bfloat16)
    contrib = jnp.einsum("khp,kn->hpn", scaled_x, b_block, preferred_element_type=jnp.float32)
    return (intra_out, cumulative, contrib)


def block_pass(x_seq, dt_seq, b_seq, c_seq, forget_rate):
    head_count, head_size = (x_seq.shape[1], x_seq.shape[2])
    state_size = b_seq.shape[1]
    block_count = x_seq.shape[0] // BLOCK
    x_blocks = x_seq.reshape(block_count, BLOCK, head_count, head_size)
    dt_blocks = dt_seq.reshape(head_count, block_count, BLOCK).transpose(1, 0, 2)
    b_blocks = b_seq.reshape(block_count, BLOCK, state_size)
    c_blocks = c_seq.reshape(block_count, BLOCK, state_size)

    def block_step(carried, inputs):
        decay_sum, running = carried
        x_block, dt_block, b_block, c_block = inputs
        intra_out, cumulative, contrib = block_terms(
            x_block, dt_block, b_block, c_block, forget_rate
        )
        record = (intra_out, cumulative, decay_sum, running)
        running = jnp.exp(cumulative[:, -1])[:, None, None] * running + contrib
        return ((decay_sum + cumulative[:, -1], running), record)

    initial = (
        jnp.zeros((head_count,), jnp.float32),
        jnp.zeros((head_count, head_size, state_size), jnp.float32),
    )
    totals, records = lax.scan(block_step, initial, (x_blocks, dt_blocks, b_blocks, c_blocks))
    return (totals, records)


def apply_state(records, c_seq, incoming):
    intra_outs, cumulatives, decay_sums, runnings = records
    block_count = intra_outs.shape[0]
    c_blocks = c_seq.reshape(block_count, BLOCK, c_seq.shape[1])

    def block_output(inputs):
        intra_out, cumulative, decay_sum, running, c_block = inputs
        held_state = (jnp.exp(decay_sum)[:, None, None] * incoming + running).astype(jnp.bfloat16)
        state_out = jnp.einsum(
            "qn,hpn->qhp", c_block, held_state, preferred_element_type=jnp.float32
        )
        return intra_out + state_out * jnp.exp(cumulative).T[:, :, None]

    outputs = lax.map(block_output, (intra_outs, cumulatives, decay_sums, runnings, c_blocks))
    return outputs.reshape(block_count * BLOCK, outputs.shape[2] * outputs.shape[3])


def chain_combine(earlier, later_pair):
    return (
        earlier[0] + later_pair[0],
        jnp.exp(later_pair[0])[:, None, None] * earlier[1] + later_pair[1],
    )


def body(
    ssm_input,
    gate_input,
    state_proj,
    step_raw,
    decay_log,
    skip_gain,
    norm_gain,
    out_weight,
    latents,
    lengths,
):
    row_count = ssm_input.shape[1]
    inner_width = ssm_input.shape[2]
    head_count = decay_log.shape[1]
    head_size = inner_width // head_count
    state_size = state_proj.shape[2] // 4
    model_width = out_weight.shape[1]
    positions = lax.axis_index("seq") * row_count + jnp.arange(row_count, dtype=jnp.int32)
    is_valid = positions < lengths[0]
    quantized_stride_width = jnp.where(is_valid[None, :], jax.nn.softplus(step_raw[0]), 0.0)
    decay_rates = jnp.exp(decay_log)
    flat_tokens = ssm_input[0]
    tokens = flat_tokens.reshape(row_count, head_count, head_size)
    projections = state_proj[0]
    forward_c = projections[:, state_size : 2 * state_size]
    backward_c = projections[::-1, 3 * state_size :]
    forward_totals, forward_records = block_pass(
        tokens,
        quantized_stride_width[:head_count],
        projections[:, :state_size],
        forward_c,
        decay_rates[0],
    )
    backward_totals, backward_records = block_pass(
        tokens[::-1],
        quantized_stride_width[head_count:, ::-1],
        projections[::-1, 2 * state_size : 3 * state_size],
        backward_c,
        decay_rates[1],
    )
    identity = (
        jnp.zeros((head_count,), jnp.float32),
        jnp.zeros((head_count, head_size, state_size), jnp.float32),
    )
    unused_item, forward_in = carried_in(
        (forward_totals[0], forward_totals[1]), "seq", chain_combine, identity, False
    )
    unused_item, backward_in = carried_in(
        (backward_totals[0], backward_totals[1]), "seq", chain_combine, identity, True
    )
    forward_out = apply_state(forward_records, forward_c, forward_in)
    backward_out = apply_state(backward_records, backward_c, backward_in)[::-1]
    skip_wide = jnp.repeat(skip_gain, head_size)
    mixed_out = forward_out + backward_out + skip_wide[None, :] * flat_tokens.astype(jnp.float32)
    gated_out = mixed_out * jax.nn.silu(gate_input[0].astype(jnp.float32))
    squared = (gated_out * gated_out).reshape(row_count, head_count, head_size)
    mean_square = jnp.mean(squared, axis=2)
    inverse_scale = jnp.repeat(lax.rsqrt(mean_square + 1e-05), head_size, axis=1)
    normed = (gated_out * inverse_scale * norm_gain[None, :]).astype(jnp.bfloat16)
    projected = jnp.dot(
        normed,
        lax.all_gather(out_weight, "dp", axis=0, tiled=True),
        preferred_element_type=jnp.float32,
    )
    encoded = projected.astype(jnp.bfloat16)
    score_scale = 1.0 / math.sqrt(model_width)
    scores = (
        jnp.einsum("rd,sd->rs", latents, encoded, preferred_element_type=jnp.float32) * score_scale
    )
    local_top = jnp.max(jnp.where(is_valid[None, :], scores, -1e30), axis=1)
    top_score = lax.pmax(local_top, "seq")
    prob_values = jnp.where(is_valid[None, :], jnp.exp(scores - top_score[:, None]), 0.0)
    weight_sum = jnp.sum(prob_values, axis=1)
    weighted_sum = jnp.dot(
        prob_values.astype(jnp.bfloat16), encoded, preferred_element_type=jnp.float32
    )
    total_weight, total_sum = (
        lax.psum(weight_sum.astype(jnp.bfloat16), "seq").astype(jnp.float32),
        lax.psum(weighted_sum.astype(jnp.bfloat16), "seq").astype(jnp.float32),
    )
    pooled = (total_sum / total_weight[:, None]).astype(jnp.bfloat16)
    return (encoded[None], pooled[None])


def solution(mesh):
    in_specs = (
        P("dp", "seq", None),
        P("dp", "seq", None),
        P("dp", "seq", None),
        P("dp", None, "seq"),
        P(),
        P(),
        P(),
        P("dp", None),
        P(),
        P("dp"),
    )
    out_specs = (P("dp", "seq", None), P("dp", None, None))
    return jax.shard_map(body, mesh=mesh, in_specs=in_specs, out_specs=out_specs, check_vma=False)
```

profile of v0, /device:TPU:0, one launch (start us, length us, event | category | flops | bytes accessed | tf_op | source)
XLA Modules:
  0.0 313.2 jit_solution(845254665929860935)
XLA Ops:
  8.9 1.0 fusion.95
  10.1 1.2 copy.26
  12.8 1.2 broadcast.82.clone
  14.0 5.1 %while.93 = (s32[]{:T(128)}, f32[16]{0:T(128)S(1)}, f32[16,64,128]{2,1,0:T(8,128)S(1)}, f32[2,128,16,64]{1,3,2,0:T(8,128)S(1)}, f32[2,16,128]{2,1,0:T(8,128)S(1)...) while((s32[]{:T(128)}, f32[16]{0:T(128)S(1)}, ...), condition=%wide.region_9.10_spmd.clone, body=%wide.region_7.9_spmd.clone.sunk | while | flops 73816096 | bytes 3535721 | solution.py:64
  15.4 0.9 bitcast_dynamic-update-slice_fusion.11
  17.9 0.9 bitcast_dynamic-update-slice_fusion.11
  20.0 1.8 reshape.184
  21.8 1.6 copy.24
  23.5 1.1 broadcast.82.clone.1
  24.6 8.9 %while.92 = (s32[]{:T(128)}, f32[16]{0:T(128)S(1)}, f32[16,64,128]{2,1,0:T(8,128)S(1)}, f32[2,128,16,64]{1,3,2,0:T(8,128)S(1)}, f32[2,16,128]{2,1,0:T(8,128)S(1)...) while((s32[]{:T(128)}, f32[16]{0:T(128)S(1)}, ...), condition=%wide.region_2.3_spmd.clone, body=%wide.region_0.2_spmd.clone.sunk | while | flops 73816096 | bytes 3535721 | solution.py:64
  25.2 1.5 fusion.143
  27.8 1.2 convolution_add_fusion.4
  29.6 1.5 fusion.143
  31.4 0.8 bitcast_dynamic-update-slice_fusion.9
  32.2 1.2 convolution_add_fusion.4
  36.8 23.4 %all-reduce.2 = (f32[128]{0:T(128)S(1)}, f32[128]{0:T(128)S(1)}) all-reduce(f32[128]{0:T(128)S(1)} %dynamic-update-slice.1, f32[128]{0:T(128)S(1)} %dynamic-update-slice), channel_id=4, replica_groups=mesh['dp'=4,'seq'=8] {'seq'}, use_global_device_ids=true, to_apply=%add.1 | all-reduce | flops 256 | bytes 2048
  60.4 2.0 copy.31
  62.6 33.9 %all-gather.12.cloned.1.call-done = f32[128,64,128]{2,1,0:T(8,128)} async-done(((f32[16,64,128]{2,1,0:T(8,128)}), f32[128,64,128]{2,1,0:T(8,128)}) %all-gather.12.cloned.1.call-update) | async-done | bytes 4194320 | tf_op jit(solution)/shard_map/all_gather | solution.py:15
  96.5 8.7 %while.90 = (s32[]{:T(128)}, f32[16,64,128]{2,1,0:T(8,128)S(1)}, s32[]{:T(128)}, f32[8,16]{1,0:T(8,128)S(1)}, f32[8,16,64,128]{3,2,1,0:T(8,128)}, /*index=5*/s32[]{:T(128)}, s32[]{:T(128)}, s32[]{:T(128)}, s32[]{:T(128)}) while((s32[]{:T(128)}, f32[16,64,128]{2,1,0:T(8,128)S(1)}, s32[]{:T(128)}, f32[8,16]{1,0:T(8,128)S(1)}, ...), condition=%wide.region_11.12_spmd, body=%wide.region_10.11_spmd.sunk | while | flops 262150 | bytes 1573203 | solution.py:24
  96.5 1.2 bitcast_add_fusion.6
  97.8 1.2 bitcast_add_fusion.6
  99.0 1.2 bitcast_add_fusion.6
  100.2 1.2 bitcast_add_fusion.6
  101.5 1.2 bitcast_add_fusion.6
  102.7 1.2 bitcast_add_fusion.6
  104.0 1.2 bitcast_add_fusion.6
  105.2 1.4 broadcast.77.clone2
  106.6 28.8 %while.91 = (s32[]{:T(128)}, f32[2,128,16,64]{1,0,3,2:T(2,128)}, f32[2,128,16,64]{1,3,2,0:T(8,128)S(1)}, bf16[2,128,128]{2,1,0:T(8,128)(2,1)S(1)}, f32[2,16]{1,0...) while((s32[]{:T(128)}, f32[2,128,16,64]{1,0,3,2:T(2,128)}, ...), condition=%wide.region_13.14_spmd, body=%wide.region_12.13_spmd.sunk | while | flops 34209792 | bytes 3205361 | solution.py:81
  106.7 1.3 fusion.135
  108.0 13.1 %dynamic_update_slice.59 = f32[2,128,16,64]{1,0,3,2:T(2,128)} dynamic-update-slice(f32[2,128,16,64]{1,0,3,2:T(2,128)} %get-tuple-element.1058, f32[1,128,16,64]{1,0,3,2:T(1,128)S(1)} %bitcast.288, s32[]{:T(128)} %get-tuple-element.1057, s32[]{:T(128)} %constant.138.clone.1..sunk.3, s32[]{:T(128)} %constant.138.clone.1..sunk.3, s32[]{:T(128)} %constant.138.clone.1..sunk.3) | dynamic-update-slice | bytes 1048580 | tf_op jit(solution)/shard_map/while/body/jit(dynamic_update_index_in_dim)/dynamic_update_slice | solution.py:64
  121.1 1.3 fusion.135
  122.4 13.1 %dynamic_update_slice.59 = f32[2,128,16,64]{1,0,3,2:T(2,128)} dynamic-update-slice(f32[2,128,16,64]{1,0,3,2:T(2,128)} %get-tuple-element.1058, f32[1,128,16,64]{1,0,3,2:T(1,128)S(1)} %bitcast.288, s32[]{:T(128)} %get-tuple-element.1057, s32[]{:T(128)} %constant.138.clone.1..sunk.3, s32[]{:T(128)} %constant.138.clone.1..sunk.3, s32[]{:T(128)} %constant.138.clone.1..sunk.3) | dynamic-update-slice | bytes 1048580 | tf_op jit(solution)/shard_map/while/body/jit(dynamic_update_index_in_dim)/dynamic_update_slice | solution.py:64
  135.5 1.3 copy.49
  136.8 5.9 %rev.19 = f32[256,1024]{0,1:T(8,128)} reverse(f32[256,1024]{0,1:T(8,128)S(1)} %bitcast.293), dimensions={0} | reverse | bytes 2097152 | tf_op jit(solution)/shard_map/rev | solution.py:144
  142.7 27.6 %all-gather.10.cloned.1.call-done = f32[128,64,128]{2,1,0:T(8,128)} async-done(((f32[16,64,128]{2,1,0:T(8,128)}), f32[128,64,128]{2,1,0:T(8,128)}) %all-gather.10.cloned.1.call-update) | async-done | bytes 4194320 | tf_op jit(solution)/shard_map/all_gather | solution.py:15
  170.3 1.4 broadcast.77.clone2.1
  171.8 28.9 %while.89 = (s32[]{:T(128)}, f32[2,128,16,64]{1,0,3,2:T(2,128)}, f32[2,128,16,64]{1,3,2,0:T(8,128)S(1)}, bf16[2,128,128]{2,1,0:T(8,128)(2,1)S(1)}, f32[2,16]{1,0...) while((s32[]{:T(128)}, f32[2,128,16,64]{1,0,3,2:T(2,128)}, ...), condition=%wide.region_6.7_spmd, body=%wide.region_5.6_spmd.sunk | while | flops 34209792 | bytes 3205361 | solution.py:81
  171.8 1.4 fusion.131
  173.2 13.1 %dynamic_update_slice.58 = f32[2,128,16,64]{1,0,3,2:T(2,128)} dynamic-update-slice(f32[2,128,16,64]{1,0,3,2:T(2,128)} %get-tuple-element.1112, f32[1,128,16,64]{1,0,3,2:T(1,128)S(1)} %bitcast.289, s32[]{:T(128)} %get-tuple-element.1111, s32[]{:T(128)} %constant.138.clone.1..sunk.1, s32[]{:T(128)} %constant.138.clone.1..sunk.1, s32[]{:T(128)} %constant.138.clone.1..sunk.1) | dynamic-update-slice | bytes 1048580 | tf_op jit(solution)/shard_map/while/body/jit(dynamic_update_index_in_dim)/dynamic_update_slice | solution.py:64
  186.3 1.3 fusion.131
  187.6 13.1 %dynamic_update_slice.58 = f32[2,128,16,64]{1,0,3,2:T(2,128)} dynamic-update-slice(f32[2,128,16,64]{1,0,3,2:T(2,128)} %get-tuple-element.1112, f32[1,128,16,64]{1,0,3,2:T(1,128)S(1)} %bitcast.289, s32[]{:T(128)} %get-tuple-element.1111, s32[]{:T(128)} %constant.138.clone.1..sunk.1, s32[]{:T(128)} %constant.138.clone.1..sunk.1, s32[]{:T(128)} %constant.138.clone.1..sunk.1) | dynamic-update-slice | bytes 1048580 | tf_op jit(solution)/shard_map/while/body/jit(dynamic_update_index_in_dim)/dynamic_update_slice | solution.py:64
  200.7 2.3 bitcast_reduce_fusion
  203.2 2.3 convolution_convert_fusion.1
  205.9 27.6 %pmax.7 = f32[256]{0:T(256)S(1)} all-reduce(f32[256]{0:T(256)S(1)} %get-tuple-element.608), channel_id=1, replica_groups=mesh['dp'=4,'seq'=8] {'seq'}, use_global_device_ids=true, to_apply=%region_16.17 | all-reduce | flops 256 | bytes 2048 | tf_op jit(solution)/shard_map/pmax | solution.py:163
  233.5 1.2 convolution_convert_fusion
  234.8 17.1 %psum.15 = bf16[256]{0:T(256)(128)(2,1)S(1)} all-reduce(bf16[256]{0:T(256)(128)(2,1)S(1)} %fusion.82), channel_id=1, replica_groups=mesh['dp'=4,'seq'=8] {'seq'}, use_global_device_ids=true, to_apply=%region_19.20 | all-reduce | flops 256 | bytes 1024 | tf_op jit(solution)/shard_map/psum | solution.py:170
  252.0 52.6 %all-reduce.5.cloned.1.call-done = bf16[256,1024]{1,0:T(8,128)(2,1)} async-done(((bf16[256,1024]{1,0:T(8,128)(2,1)}), bf16[256,1024]{1,0:T(8,128)(2,1)}) %all-reduce.5.cloned.1.call-update) | async-done | bytes 524304 | tf_op jit(solution)/shard_map/psum | solution.py:171
  304.6 2.1 fusion.81
  (130 shorter events, 13.3 us)
Async XLA Ops:
  7.2 198.4 %copy-start = (bf16[256,1024]{1,0:T(8,128)(2,1)S(1)}, bf16[256,1024]{1,0:T(8,128)(2,1)}, u32[]{:S(2)}) copy-start(bf16[256,1024]{1,0:T(8,128)(2,1)} %param.30) | copy-start | bytes 1572868
  7.2 89.2 %all-gather.12.cloned.1.call-start = ((), (), s32[]{:S(2)}) async-start(), calls=%async_computation.3 | async-start | bytes 4718592 | tf_op jit(solution)/shard_map/all_gather | solution.py:15
  11.4 1.3 copy-start.5
  19.1 0.8 copy-start.1
  19.9 150.3 %all-gather.10.cloned.1.call-start = ((), (), s32[]{:S(2)}) async-start(), calls=%async_computation.2 | async-start | bytes 4718592 | tf_op jit(solution)/shard_map/all_gather | solution.py:15
  24.6 10.5 %copy-start.10 = (u32[32]{0:T(128)S(1)}, u32[32]{0:T(128)}, u32[]{:S(2)}) copy-start(u32[32]{0:T(128)} %constant.156) | copy-start | bytes 388
  24.6 37.8 %copy-start.9 = (f32[16]{0:T(128)S(1)}, f32[16]{0:T(128)}, u32[]{:S(2)}) copy-start(f32[16]{0:T(128)} %param.27) | copy-start | bytes 196
  33.5 0.8 copy-start.2
  33.5 63.0 %copy-start.3 = (f32[2,128,16,64]{1,3,2,0:T(8,128)}, f32[2,128,16,64]{1,3,2,0:T(8,128)S(1)}, u32[]{:S(2)}) copy-start(f32[2,128,16,64]{1,3,2,0:T(8,128)S(1)} %get-tuple-element.1103) | copy-start | bytes 3145732
  34.3 168.9 %all-gather.8.cloned.1.call-start = ((), (), s32[]{:S(2)}) async-start(), calls=%async_computation | async-start | bytes 2621440 | tf_op jit(solution)/shard_map/all_gather | solution.py:154
  35.0 269.6 %all-reduce.5.cloned.1.call-start = ((), (), s32[]{:S(2)}) async-start(), calls=%async_computation.1 | async-start | bytes 1048576 | tf_op jit(solution)/shard_map/psum | solution.py:171
  170.3 1.5 copy-start.4
  171.8 28.9 %copy-start.6 = (bf16[1,256,1024]{1,2,0:T(8,128)(2,1)S(1)}, bf16[1,256,1024]{1,2,0:T(8,128)(2,1)}, u32[]{:S(2)}) copy-start(bf16[1,256,1024]{1,2,0:T(8,128)(2,1)} %copy-done.5) | copy-start | bytes 1572868
  200.7 2.3 copy-start.8
  205.6 101.1 %copy-start.7 = (bf16[256,1024]{1,0:T(8,128)(2,1)}, bf16[256,1024]{1,0:T(8,128)(2,1)S(1)}, u32[]{:S(2)}) copy-start(bf16[256,1024]{1,0:T(8,128)(2,1)S(1)} %convolution_convert_fusion.1) | copy-start | bytes 1572868
Sparse Core Ops, SparseCore 0:
  20.0 76.3 all-gather.11
  98.5 71.6 all-gather.9
  171.8 20.8 all-gather.7
  234.9 69.7 all-reduce.4
where the time goes:
time: 318 us; the launch traced here: 313 us
  waiting for transfers between devices  115 us (36%)
  local copies, waits for them, and re-layouts  78.2 us (25%)
  blocking collectives  68.1 us (21%)
  other arithmetic  19.2 us (6%)
  matrix products  16.7 us (5%)
  between operations  15.4 us (5%)
    all_gather x2, waiting for transfers between devices, carried_in(): gathered = jax.tree.map(lambda a: lax.all_gather(a, axis), part)  61.4 us
    psum x1, waiting for transfers between devices, body(): lax.psum(weighted_sum.astype(jnp.bfloat16), 'seq').astype(jnp.float32)  52.6 us
    dynamic_update_slice x12, local copies, waits for them, and re-layouts, block_pass(): lax.scan(block_step, initial, (x_blocks, dt_blocks, b_blocks, c_blocks))  52.4 us
    pmax x1, blocking collectives, body(): top_score = lax.pmax(local_top, 'seq')  27.6 us
    unnamed x1, blocking collectives  23.4 us
    psum x1, blocking collectives, body(): lax.psum(weight_sum.astype(jnp.bfloat16), 'seq').astype(jnp.float32)  17.1 us
    unnamed x32, local copies, waits for them, and re-layouts  8.97 us
    add x7, other arithmetic, chain_combine(): jnp.exp(later_pair[0])[:, None, None] * earlier[1] + later_pair[1]  8.37 us
  transfers between devices with their start and end apart: 4, of which 3 were waited for; matrix products, arithmetic and copies ran while one was open for 31% of the time, Pallas kernels for 0%

commit v1 on v0

v1 whole, which is shorter than its diff:
```python
import functools
import math

import jax
import jax.numpy as jnp
from jax import lax
from jax.experimental import pallas as pl
from jax.experimental.pallas import tpu as pltpu
from jax.sharding import PartitionSpec as P

CHUNK = 256
PAIR = 128
F32 = jnp.float32
BF16 = jnp.bfloat16


def dot(a, b, dims=((1,), (0,)), precision=None):
    return lax.dot_general(
        a, b, (dims, ((), ())), precision=precision, preferred_element_type=F32
    )


def column_of(row, size):
    eye = lax.broadcasted_iota(jnp.int32, (size, size), 0) == lax.broadcasted_iota(
        jnp.int32, (size, size), 1
    )
    return jnp.sum(jnp.where(eye, jnp.broadcast_to(row, (size, size)), 0.0), axis=1, keepdims=True)


def kernel(
    n,
    n_dp,
    lengths,
    skip,
    x_ref,
    gate_ref,
    proj_ref,
    raw_ref,
    decay_ref,
    gain_ref,
    w_ref,
    latents_ref,
    enc_ref,
    pooled_ref,
    w_all,
    own_state,
    own_decay,
    state_send,
    pair_in,
    chain_in,
    chain_out,
    leaf_in,
    incoming,
    head_out,
    factor,
    normed,
    sum_send,
    stat_send,
    sum_recv,
    stat_recv,
    pool,
    w_send_sem,
    w_fwd_sem,
    w_recv_sem,
    pair_send_sem,
    pair_recv_sem,
    chain_send_sem,
    chain_recv_sem,
    leaf_send_sem,
    leaf_recv_sem,
    sum_send_sem,
    sum_recv_sem,
    stat_send_sem,
    stat_recv_sem,
    pool_send_sem,
    pool_recv_sem,
):
    rows, width = x_ref.shape[1], x_ref.shape[2]
    heads = decay_ref.shape[1]
    head_size = width // heads
    state = proj_ref.shape[2] // 4
    chunks = width // CHUNK
    w_rows = w_ref.shape[0]
    me = lax.axis_index("seq")
    my_dp = lax.axis_index("dp")

    def remote(src, dst, send_sem, recv_sem, seq=None, dp=None):
        device_id = {"seq": seq} if dp is None else {"dp": dp}
        return pltpu.make_async_remote_copy(
            src_ref=src,
            dst_ref=dst,
            send_sem=send_sem,
            recv_sem=recv_sem,
            device_id=device_id,
            device_id_type=pl.DeviceIdType.MESH,
        )

    side = lax.rem(me, 2)
    place = me // 2
    places = n // 2
    partner = me + 1 - 2 * side
    node_dir = 1 - side
    along = jnp.where(side == 1, place, places - 1 - place)
    leaf_along = jnp.where(side == 1, places - 1 - place, place)
    following = lax.rem(me + 4 * side - 2 + n, n)
    core = lax.rem(my_dp, 2)
    dp_partner = my_dp + 1 - 2 * core

    barrier = pltpu.get_barrier_semaphore()
    for step in range(1, n):
        pl.semaphore_signal(
            barrier,
            inc=1,
            device_id={"seq": lax.rem(me + step, n)},
            device_id_type=pl.DeviceIdType.MESH,
        )
    pl.semaphore_signal(
        barrier, inc=1, device_id={"dp": dp_partner}, device_id_type=pl.DeviceIdType.MESH
    )
    for step in range(2, n_dp, 2):
        pl.semaphore_signal(
            barrier,
            inc=1,
            device_id={"dp": lax.rem(my_dp + step, n_dp)},
            device_id_type=pl.DeviceIdType.MESH,
        )
    pl.semaphore_wait(barrier, n - 1 + n_dp // 2)

    def w_slot(owner):
        return w_all.at[pl.ds(pl.multiple_of(owner * w_rows, w_rows), w_rows)]

    w_copies = []
    for step in range(2, n_dp, 2):
        w_copies.append(
            remote(
                w_ref,
                w_slot(my_dp),
                w_send_sem.at[step],
                w_recv_sem.at[step],
                dp=lax.rem(my_dp + step, n_dp),
            )
        )
    w_copies.append(
        remote(w_ref, w_slot(my_dp), w_send_sem.at[0], w_recv_sem.at[0], dp=dp_partner)
    )
    for copy in w_copies:
        copy.start()

    token = lax.broadcasted_iota(jnp.int32, (1, rows), 1)
    valid = (me * rows + token) < lengths[0]
    raw = raw_ref[0]
    softplus = jnp.maximum(raw, 0.0) + jnp.log1p(jnp.exp(-jnp.abs(raw)))
    dt = jnp.where(valid, softplus, 0.0)
    rates = jnp.exp(decay_ref[...])
    step_f, step_b = dt[:heads], dt[heads:]
    loss_f = -step_f * column_of(rates[0:1], heads)
    loss_b = -step_b * column_of(rates[1:2], heads)
    row_at = lax.broadcasted_iota(jnp.int32, (rows, rows), 0)
    col_at = lax.broadcasted_iota(jnp.int32, (rows, rows), 1)
    cum_f = dot(loss_f, jnp.where(row_at <= col_at, 1.0, 0.0), precision=lax.Precision.HIGHEST)
    cum_b = dot(loss_b, jnp.where(row_at >= col_at, 1.0, 0.0), precision=lax.Precision.HIGHEST)
    stacked = jnp.concatenate(
        [cum_f, cum_b, step_f, step_b, jnp.zeros((128 - 4 * heads, rows), F32)], axis=0
    )
    by_token = stacked.T
    col_f, col_b = by_token[:, :heads], by_token[:, heads : 2 * heads]
    dt_f, dt_b = by_token[:, 2 * heads : 3 * heads], by_token[:, 3 * heads : 4 * heads]
    tail_f = jnp.exp(col_f[rows - 1 : rows] - col_f) * dt_f
    tail_b = jnp.exp(col_b[0:1] - col_b) * dt_b
    grow_f, grow_b = jnp.exp(col_f), jnp.exp(col_b)

    head_row = lax.broadcasted_iota(jnp.int32, (heads, width), 0) * head_size
    head_lane = lax.broadcasted_iota(jnp.int32, (heads, width), 1)
    spread = jnp.where(
        (head_lane >= head_row) & (head_lane < head_row + head_size), 1.0, 0.0
    ).astype(BF16)

    def split(values):
        high = values.astype(BF16)
        return high, (values - high.astype(F32)).astype(BF16)

    def widen(parts, c):
        columns = spread[:, c * CHUNK : (c + 1) * CHUNK]
        return dot(parts[0], columns) + dot(parts[1], columns)

    proj = proj_ref[0]
    b_f, c_f = proj[:, :state], proj[:, state : 2 * state]
    b_b, c_b = proj[:, 2 * state : 3 * state], proj[:, 3 * state :]

    tails = (split(tail_f), split(tail_b))
    grows = (split(grow_f), split(grow_b))
    for c in range(chunks):
        columns = slice(c * CHUNK, (c + 1) * CHUNK)
        x_chunk = x_ref[0, :, columns].astype(F32)
        for d, b_d in ((0, b_f), (1, b_b)):
            scaled = (x_chunk * widen(tails[d], c)).astype(BF16)
            total = dot(b_d, scaled, ((0,), (0,)))
            grow = widen(grows[d], c)
            factor[d, :, columns] = grow
            decay = grow[rows - 1 : rows] if d == 0 else grow[0:1]
            own_state[d, c] = total
            own_decay[d, c] = jnp.broadcast_to(decay, (8, CHUNK))
            state_send[d, c, :state] = total.astype(BF16)
            high, low = split(decay)
            state_send[d, c, state:] = jnp.where(
                lax.broadcasted_iota(jnp.int32, (16, CHUNK), 0) == 0,
                high.astype(F32),
                jnp.where(
                    lax.broadcasted_iota(jnp.int32, (16, CHUNK), 0) == 1, low.astype(F32), 0.0
                ),
            ).astype(BF16)
        remote(
            state_send.at[side, c],
            pair_in.at[c],
            pair_send_sem.at[c],
            pair_recv_sem.at[c],
            seq=partner,
        ).start()

    gram_f = dot(c_f, b_f, ((1,), (1,)))
    gram_b = dot(c_b, b_b, ((1,), (1,)))
    earlier = col_at < row_at
    gram = jnp.where(earlier, gram_f, jnp.where(col_at == row_at, 0.0, gram_b))
    self_f = jnp.sum(c_f.astype(F32) * b_f.astype(F32), axis=1, keepdims=True)
    self_b = jnp.sum(c_b.astype(F32) * b_b.astype(F32), axis=1, keepdims=True)
    lane = lax.broadcasted_iota(jnp.int32, (rows, PAIR), 1)

    def own_part(first_pair, last_pair):
        for pair in range(first_pair, last_pair):
            columns = slice(pair * PAIR, (pair + 1) * PAIR)
            x_pair = x_ref[0, :, columns]
            result = None
            direct = None
            for k in range(PAIR // head_size):
                h = pair * (PAIR // head_size) + k
                gap = jnp.where(
                    earlier,
                    col_f[:, h : h + 1] - cum_f[h : h + 1],
                    col_b[:, h : h + 1] - cum_b[h : h + 1],
                )
                weight = jnp.where(earlier, step_f[h : h + 1], step_b[h : h + 1])
                mixing = (gram * jnp.exp(gap) * weight).astype(BF16)
                mine = (lane >= k * head_size) & (lane < (k + 1) * head_size)
                part = dot(mixing, jnp.where(mine, x_pair, jnp.zeros_like(x_pair)))
                own = self_f * dt_f[:, h : h + 1] + self_b * dt_b[:, h : h + 1] + skip[h]
                result = part if result is None else result + part
                own = jnp.broadcast_to(own, (rows, PAIR))
                direct = own if direct is None else jnp.where(mine, own, direct)
            head_out[:, columns] = result + direct * x_pair.astype(F32)

    own_part(0, width // PAIR)

    def chain_copy(c):
        return remote(
            chain_out.at[c],
            chain_in.at[c],
            chain_send_sem.at[c],
            chain_recv_sem.at[c],
            seq=following,
        )

    def leaf_copy(c):
        return remote(
            chain_in.at[c],
            leaf_in.at[c],
            leaf_send_sem.at[c],
            leaf_recv_sem.at[c],
            seq=partner,
        )

    def pair_copy(c):
        return remote(
            state_send.at[side, c],
            pair_in.at[c],
            pair_send_sem.at[c],
            pair_recv_sem.at[c],
            seq=partner,
        )

    @pl.when(along == 0)
    def _():
        chain_in[...] = jnp.zeros_like(chain_in)

    @pl.when(leaf_along == 0)
    def _():
        leaf_in[...] = jnp.zeros_like(leaf_in)

    for c in range(chunks):
        pair_copy(c).wait_recv()
        pair_state = pair_in[c, :state].astype(F32)
        pair_tail = pair_in[c, state:].astype(F32)
        pair_decay = pair_tail[0:1] + pair_tail[1:2]
        my_decay = own_decay[node_dir, c][0:1]

        @pl.when(along > 0)
        def _():
            chain_copy(c).wait_recv()
            leaf_copy(c).start()

        entering = pair_decay * chain_in[c].astype(F32) + pair_state
        incoming[node_dir, c] = entering.astype(BF16)

        @pl.when(along < places - 1)
        def _():
            chain_out[c] = (my_decay * entering + own_state[node_dir, c]).astype(BF16)
            chain_copy(c).start()

    w_all[pl.ds(pl.multiple_of(my_dp * w_rows, w_rows), w_rows)] = w_ref[...]
    forwards = []
    for i, step in enumerate(range(2, n_dp, 2)):
        w_copies[i].wait_recv()
        owner = lax.rem(my_dp + n_dp - step, n_dp)
        forward = remote(
            w_slot(owner),
            w_slot(owner),
            w_fwd_sem.at[step],
            w_recv_sem.at[step + 1],
            dp=dp_partner,
        )
        forward.start()
        forwards.append(forward)

    for c in range(chunks):
        columns = slice(c * CHUNK, (c + 1) * CHUNK)

        @pl.when(leaf_along > 0)
        def _():
            leaf_copy(c).wait_recv()

        incoming[side, c] = leaf_in[c]
        mixed = (
            head_out[:, columns]
            + dot(c_f, incoming[0, c]) * factor[0, :, columns]
            + dot(c_b, incoming[1, c]) * factor[1, :, columns]
        )
        gate = gate_ref[0, :, columns].astype(F32)
        gated = mixed * (gate / (1.0 + jnp.exp(-gate)))
        spread_chunk = spread[:, columns]
        square = split(gated * gated)
        mean = (
            dot(square[0], spread_chunk, ((1,), (1,))) + dot(square[1], spread_chunk, ((1,), (1,)))
        ) * (1.0 / head_size)
        scale = widen(split(lax.rsqrt(mean + 1e-05)), c)
        normed[:, columns] = (gated * scale * gain_ref[:, columns]).astype(BF16)

    w_copies[-1].wait_recv()
    for copy in forwards:
        copy.wait_recv()
    for c in range(chunks):
        columns = slice(c * CHUNK, (c + 1) * CHUNK)
        enc_ref[0, :, columns] = dot(normed[...], w_all[:, columns]).astype(BF16)

    encoded = enc_ref[0]
    scores = dot(latents_ref[...], encoded, ((1,), (1,))) * (1.0 / math.sqrt(encoded.shape[1]))
    top = jnp.max(jnp.where(valid, scores, -1e30), axis=1, keepdims=True)
    prob = jnp.where(valid, jnp.exp(scores - top), 0.0)
    weight_sum = jnp.sum(prob, axis=1, keepdims=True)
    queries = latents_ref.shape[0]
    share = queries // n
    half = lax.broadcasted_iota(jnp.int32, (queries, 128), 1) < 64
    stat_send[...] = jnp.where(half, top, weight_sum).reshape(n, share, 128)
    prob_low = prob.astype(BF16)
    for c in range(encoded.shape[1] // CHUNK):
        columns = slice(c * CHUNK, (c + 1) * CHUNK)
        part = dot(prob_low, encoded[:, columns])
        sum_send[:, :, columns] = part.reshape(n, share, CHUNK).astype(BF16)

    sum_copies, stat_copies = [], []
    for step in range(1, n):
        target = lax.rem(me + step, n)
        stat_copies.append(
            remote(
                stat_send.at[target],
                stat_recv.at[step],
                stat_send_sem.at[step],
                stat_recv_sem.at[step],
                seq=target,
            )
        )
        sum_copies.append(
            remote(
                sum_send.at[target],
                sum_recv.at[step],
                sum_send_sem.at[step],
                sum_recv_sem.at[step],
                seq=target,
            )
        )
    for copy in stat_copies:
        copy.start()
    for copy in sum_copies:
        copy.start()
    stat_recv[0] = stat_send[me]
    for copy in stat_copies:
        copy.wait_recv()
    tops = [stat_recv[step][:, 0:1] for step in range(n)]
    best = functools.reduce(jnp.maximum, tops)
    scales = [jnp.exp(t - best) for t in tops]
    whole = functools.reduce(
        jnp.add, [stat_recv[step][:, 64:65] * scales[step] for step in range(n)]
    )
    inverse = 1.0 / whole
    total = sum_send[me].astype(F32) * (scales[0] * inverse)
    for step in range(1, n):
        sum_copies[step - 1].wait_recv()
        total = total + sum_recv[step].astype(F32) * (scales[step] * inverse)
    pool[me] = total.astype(BF16)
    pool_copies = []
    for step in range(1, n):
        target = lax.rem(me + step, n)
        copy = remote(
            pool.at[me],
            pool.at[me],
            pool_send_sem.at[step],
            pool_recv_sem.at[step],
            seq=target,
        )
        copy.start()
        pool_copies.append(copy)
    for copy in pool_copies:
        copy.wait_recv()
    pooled_ref[0] = pool[...].reshape(queries, pool.shape[2])

    for copy in w_copies + forwards + sum_copies + stat_copies + pool_copies:
        copy.wait_send()
    for c in range(chunks):
        pair_copy(c).wait_send()

        @pl.when(along < places - 1)
        def _():
            chain_copy(c).wait_send()

        @pl.when(along > 0)
        def _():
            leaf_copy(c).wait_send()


def body(
    n,
    n_dp,
    ssm_input,
    gate_input,
    state_proj,
    step_raw,
    decay_log,
    skip_gain,
    norm_gain,
    out_weight,
    latents,
    lengths,
):
    rows, width = ssm_input.shape[1], ssm_input.shape[2]
    model = out_weight.shape[1]
    state = state_proj.shape[2] // 4
    queries = latents.shape[0]
    share = queries // n
    chunks = width // CHUNK
    vmem = pl.BlockSpec(memory_space=pltpu.VMEM)
    smem = pl.BlockSpec(memory_space=pltpu.SMEM)
    dma = pltpu.SemaphoreType.DMA
    return pl.pallas_call(
        functools.partial(kernel, n, n_dp),
        out_shape=(
            jax.ShapeDtypeStruct((1, rows, model), BF16),
            jax.ShapeDtypeStruct((1, queries, model), BF16),
        ),
        in_specs=[smem, smem] + [vmem] * 8,
        out_specs=(vmem, vmem),
        scratch_shapes=[
            pltpu.VMEM((width, model), BF16),
            pltpu.VMEM((2, chunks, state, CHUNK), F32),
            pltpu.VMEM((2, chunks, 8, CHUNK), F32),
            pltpu.VMEM((2, chunks, state + 16, CHUNK), BF16),
            pltpu.VMEM((chunks, state + 16, CHUNK), BF16),
            pltpu.VMEM((chunks, state, CHUNK), BF16),
            pltpu.VMEM((chunks, state, CHUNK), BF16),
            pltpu.VMEM((chunks, state, CHUNK), BF16),
            pltpu.VMEM((2, chunks, state, CHUNK), BF16),
            pltpu.VMEM((rows, width), F32),
            pltpu.VMEM((2, rows, width), F32),
            pltpu.VMEM((rows, width), BF16),
            pltpu.VMEM((n, share, model), BF16),
            pltpu.VMEM((n, share, 128), F32),
            pltpu.VMEM((n, share, model), BF16),
            pltpu.VMEM((n, share, 128), F32),
            pltpu.VMEM((n, share, model), BF16),
            dma((n_dp,)),
            dma((n_dp,)),
            dma((n_dp,)),
            dma((chunks,)),
            dma((chunks,)),
            dma((chunks,)),
            dma((chunks,)),
            dma((chunks,)),
            dma((chunks,)),
            dma((n,)),
            dma((n,)),
            dma((n,)),
            dma((n,)),
            dma((n,)),
            dma((n,)),
        ],
        compiler_params=pltpu.CompilerParams(
            collective_id=0, has_side_effects=True, vmem_limit_bytes=48 * 1024 * 1024
        ),
    )(
        lengths,
        skip_gain,
        ssm_input,
        gate_input,
        state_proj,
        step_raw,
        decay_log,
        norm_gain.reshape(1, width),
        out_weight,
        latents,
    )


def solution(mesh):
    in_specs = (
        P("dp", "seq", None),
        P("dp", "seq", None),
        P("dp", "seq", None),
        P("dp", None, "seq"),
        P(),
        P(),
        P(),
        P("dp", None),
        P(),
        P("dp"),
    )
    out_specs = (P("dp", "seq", None), P("dp", None, None))
    return jax.shard_map(
        functools.partial(body, mesh.shape["seq"], mesh.shape["dp"]),
        mesh=mesh,
        in_specs=in_specs,
        out_specs=out_specs,
        check_vma=False,
    )
```

time: 318 us -> 62.9 us (0.20); the launches traced: 313 us -> 62.3 us
  waiting for transfers between devices: 115 us -> 0 us
  local copies, waits for them, and re-layouts: 78.2 us -> 8.81 us
  blocking collectives: 68.1 us -> 0 us
  Pallas kernels: 0 us -> 52.2 us
  other arithmetic: 19.2 us -> 0 us
  matrix products: 16.7 us -> 0 us
  between operations: 15.4 us -> 1.31 us
    all_gather x3 -> x0, waiting for transfers between devices: 61.4 us -> none  [the longest x2 61.4 us: carried_in(): gathered = jax.tree.map(lambda a: lax.all_gather(a, axis), part)]
    psum x1 -> x0, waiting for transfers between devices: 52.6 us -> none  [body(): lax.psum(weighted_sum.astype(jnp.bfloat16), 'seq').astype(jnp.float32)]
    dynamic_update_slice x12 -> x0, local copies, waits for them, and re-layouts: 52.4 us -> none  [block_pass(): lax.scan(block_step, initial, (x_blocks, dt_blocks, b_blocks, c_blocks))]
    pallas_call x0 -> x1, Pallas kernels: none -> 52.2 us  [body(): pl.pallas_call(functools.partial(kernel, n, n_dp), out_shape=(jax.ShapeDt...]
    pmax x1 -> x0, blocking collectives: 27.6 us -> none  [body(): top_score = lax.pmax(local_top, 'seq')]
    unnamed x1 -> x0, blocking collectives: 23.4 us -> none
    psum x1 -> x0, blocking collectives: 17.1 us -> none  [body(): lax.psum(weight_sum.astype(jnp.bfloat16), 'seq').astype(jnp.float32)]
    dot_general x19 -> x0, matrix products: 16.7 us -> none  [the longest x4 5.36 us: block_output(): jnp.einsum('qn,hpn->qhp', c_block, held_state, preferred_element_type=jnp...]
  transfers between devices with their start and end apart: 4 -> 0, of which waited for: 3 -> 0; matrix products, arithmetic and copies ran while one was open for 31% -> 0% of each run, Pallas kernels for 0% -> 0%
where the time goes in v1:
time: 62.9 us; the launch traced here: 62.3 us
  Pallas kernels  52.2 us (83%)
  local copies, waits for them, and re-layouts  8.81 us (14%)
  between operations  1.31 us (2%)
    pallas_call x1, Pallas kernels, body(): pl.pallas_call(functools.partial(kernel, n, n_dp), out_shape=(jax.ShapeDt...  52.2 us
    unnamed x20, local copies, waits for them, and re-layouts  8.81 us

profile of v1, /device:TPU:0, one launch (start us, length us, event | category | flops | bytes accessed | tf_op | source)
XLA Modules:
  0.0 62.3 jit_solution(5334810570126766369)
XLA Ops:
  1.3 0.0 copy-start.7
  1.3 0.0 copy-start.8
  1.3 0.7 %copy-done.7 = f32[2,16]{1,0:T(2,128)S(1)} copy-done((f32[2,16]{1,0:T(2,128)S(1)}, f32[2,16]{1,0:T(2,128)}, u32[]{:S(2)}) %copy-start.7) | copy-done | bytes 152
  2.0 0.0 copy-done.8
  2.0 0.0 copy-start
  2.0 1.0 %copy-done = bf16[1,256,1024]{2,1,0:T(8,128)(2,1)S(1)} copy-done((bf16[1,256,1024]{2,1,0:T(8,128)(2,1)S(1)}, bf16[1,256,1024]{2,1,0:T(8,128)(2,1)}, u32[]{:S(2)}) %copy-start) | copy-done | bytes 524312
  3.0 0.0 copy-start.1
  3.0 1.0 %copy-done.1 = bf16[1,256,1024]{2,1,0:T(8,128)(2,1)S(1)} copy-done((bf16[1,256,1024]{2,1,0:T(8,128)(2,1)S(1)}, bf16[1,256,1024]{2,1,0:T(8,128)(2,1)}, u32[]{:S(2)}) %copy-start.1) | copy-done | bytes 524312
  4.0 0.0 copy-start.2
  4.0 1.0 %copy-done.2 = bf16[256,1024]{1,0:T(8,128)(2,1)S(1)} copy-done((bf16[256,1024]{1,0:T(8,128)(2,1)S(1)}, bf16[256,1024]{1,0:T(8,128)(2,1)}, u32[]{:S(2)}) %copy-start.2) | copy-done | bytes 524312
  5.1 0.0 copy-start.3
  5.1 1.0 %copy-done.3 = bf16[256,1024]{1,0:T(8,128)(2,1)S(1)} copy-done((bf16[256,1024]{1,0:T(8,128)(2,1)S(1)}, bf16[256,1024]{1,0:T(8,128)(2,1)}, u32[]{:S(2)}) %copy-start.3) | copy-done | bytes 524312
  6.1 0.0 copy-start.4
  6.1 0.9 %copy-done.4 = bf16[1,256,512]{2,1,0:T(8,128)(2,1)S(1)} copy-done((bf16[1,256,512]{2,1,0:T(8,128)(2,1)S(1)}, bf16[1,256,512]{2,1,0:T(8,128)(2,1)}, u32[]{:S(2)}) %copy-start.4) | copy-done | bytes 262168
  7.1 0.0 copy-start.5
  7.1 0.8 %copy-done.5 = f32[1,32,256]{2,1,0:T(8,128)S(1)} copy-done((f32[1,32,256]{2,1,0:T(8,128)S(1)}, f32[1,32,256]{2,1,0:T(8,128)}, u32[]{:S(2)}) %copy-start.5) | copy-done | bytes 32792
  7.8 0.0 copy-start.6
  7.8 0.7 %copy-done.6 = f32[1024]{0:T(1024)S(1)} copy-done((f32[1024]{0:T(1024)S(1)}, f32[1024]{0:T(1024)}, u32[]{:S(2)}) %copy-start.6) | copy-done | bytes 4120
  8.5 52.2 %shard_map.113 = (bf16[1,256,1024]{2,1,0:T(8,128)(2,1)S(1)}, bf16[1,256,1024]{2,1,0:T(8,128)(2,1)S(1)}) custom-call(s32[1]{0:T(128)S(6)} %copy.14.lengths, f32[16]{0:T(128)S(1)} %copy-done.8, bf16[1,256,1024]{2,1,0:T(8,128)(2,1)S(1)} %copy-done, bf16[1,256,1024]{2,1,0:T(8,128)(2,1)S(1)} %copy-done.1, bf16[1,256,512]{2,1,0:T(8,128)(2,1)S(1)} %copy-done.4, ...), custom_call_target="tpu_custom_call" | custom-call | tf_op jit(solution)/shard_map/pallas_call | solution.py:461
  60.7 0.8 %copy.15 = bf16[1,256,1024]{2,1,0:T(8,128)(2,1)} copy(bf16[1,256,1024]{2,1,0:T(8,128)(2,1)S(1)} %get-tuple-element.4) | data formatting | bytes 1048576
  61.5 0.8 %copy.16 = bf16[1,256,1024]{2,1,0:T(8,128)(2,1)} copy(bf16[1,256,1024]{2,1,0:T(8,128)(2,1)S(1)} %get-tuple-element.5) | data formatting | bytes 1048576
Async XLA Ops:
  1.3 0.7 %copy-start.7 = (f32[2,16]{1,0:T(2,128)S(1)}, f32[2,16]{1,0:T(2,128)}, u32[]{:S(2)}) copy-start(f32[2,16]{1,0:T(2,128)} %decay_ref.1) | copy-start | bytes 388
  1.3 0.7 %copy-start.8 = (f32[16]{0:T(128)S(1)}, f32[16]{0:T(128)}, u32[]{:S(2)}) copy-start(f32[16]{0:T(128)} %skip.1) | copy-start | bytes 196
  2.0 1.0 %copy-start = (bf16[1,256,1024]{2,1,0:T(8,128)(2,1)S(1)}, bf16[1,256,1024]{2,1,0:T(8,128)(2,1)}, u32[]{:S(2)}) copy-start(bf16[1,256,1024]{2,1,0:T(8,128)(2,1)} %x_ref.1) | copy-start | bytes 1572868
  3.0 1.0 %copy-start.1 = (bf16[1,256,1024]{2,1,0:T(8,128)(2,1)S(1)}, bf16[1,256,1024]{2,1,0:T(8,128)(2,1)}, u32[]{:S(2)}) copy-start(bf16[1,256,1024]{2,1,0:T(8,128)(2,1)} %gate_ref.1) | copy-start | bytes 1572868
  4.0 1.0 %copy-start.2 = (bf16[256,1024]{1,0:T(8,128)(2,1)S(1)}, bf16[256,1024]{1,0:T(8,128)(2,1)}, u32[]{:S(2)}) copy-start(bf16[256,1024]{1,0:T(8,128)(2,1)} %w_ref.1) | copy-start | bytes 1572868
  5.1 1.0 %copy-start.3 = (bf16[256,1024]{1,0:T(8,128)(2,1)S(1)}, bf16[256,1024]{1,0:T(8,128)(2,1)}, u32[]{:S(2)}) copy-start(bf16[256,1024]{1,0:T(8,128)(2,1)} %latents_ref.1) | copy-start | bytes 1572868
  6.1 0.9 %copy-start.4 = (bf16[1,256,512]{2,1,0:T(8,128)(2,1)S(1)}, bf16[1,256,512]{2,1,0:T(8,128)(2,1)}, u32[]{:S(2)}) copy-start(bf16[1,256,512]{2,1,0:T(8,128)(2,1)} %proj_ref.1) | copy-start | bytes 786436
  7.1 0.8 %copy-start.5 = (f32[1,32,256]{2,1,0:T(8,128)S(1)}, f32[1,32,256]{2,1,0:T(8,128)}, u32[]{:S(2)}) copy-start(f32[1,32,256]{2,1,0:T(8,128)} %raw_ref.1) | copy-start | bytes 98308
  7.8 0.7 %copy-start.6 = (f32[1024]{0:T(1024)S(1)}, f32[1024]{0:T(1024)}, u32[]{:S(2)}) copy-start(f32[1024]{0:T(1024)} %param.16) | copy-start | bytes 12292

commit v2 on v1

--- a/solution.py
+++ b/solution.py
@@ -32,16 +32,25 @@
     n_dp,
     lengths,
     skip,
+    x_hbm,
+    gate_hbm,
+    proj_hbm,
+    raw_hbm,
+    decay_hbm,
+    gain_hbm,
+    w_ref,
+    latents_hbm,
+    enc_ref,
+    pooled_ref,
     x_ref,
     gate_ref,
     proj_ref,
     raw_ref,
     decay_ref,
     gain_ref,
-    w_ref,
     latents_ref,
-    enc_ref,
-    pooled_ref,
+    silu,
+    load_sem,
     w_all,
     own_state,
     own_decay,
@@ -106,6 +115,24 @@
     core = lax.rem(my_dp, 2)
     dp_partner = my_dp + 1 - 2 * core
 
+    loads = [
+        pltpu.make_async_copy(source, target, load_sem.at[i])
+        for i, (source, target) in enumerate(
+            (
+                (raw_hbm, raw_ref),
+                (decay_hbm, decay_ref),
+                (proj_hbm, proj_ref),
+                (x_hbm, x_ref),
+                (gate_hbm, gate_ref),
+                (gain_hbm, gain_ref),
+                (latents_hbm, latents_ref),
+                (w_ref, w_all.at[pl.ds(pl.multiple_of(my_dp * w_rows, w_rows), w_rows)]),
+            )
+        )
+    ]
+    for load in loads:
+        load.start()
+
     barrier = pltpu.get_barrier_semaphore()
     for step in range(1, n):
         pl.semaphore_signal(
@@ -145,6 +172,9 @@
     )
     for copy in w_copies:
         copy.start()
+
+    for load in loads[:4]:
+        load.wait()
 
     token = lax.broadcasted_iota(jnp.int32, (1, rows), 1)
     valid = (me * rows + token) < lengths[0]
@@ -189,25 +219,26 @@
 
     tails = (split(tail_f), split(tail_b))
     grows = (split(grow_f), split(grow_b))
+    ends = (
+        split(jnp.broadcast_to(grow_f[rows - 1 : rows], (8, heads))),
+        split(jnp.broadcast_to(grow_b[0:1], (8, heads))),
+    )
+    tail_row = lax.broadcasted_iota(jnp.int32, (16, CHUNK), 0)
     for c in range(chunks):
         columns = slice(c * CHUNK, (c + 1) * CHUNK)
         x_chunk = x_ref[0, :, columns].astype(F32)
         for d, b_d in ((0, b_f), (1, b_b)):
             scaled = (x_chunk * widen(tails[d], c)).astype(BF16)
             total = dot(b_d, scaled, ((0,), (0,)))
-            grow = widen(grows[d], c)
-            factor[d, :, columns] = grow
-            decay = grow[rows - 1 : rows] if d == 0 else grow[0:1]
+            decay = widen(ends[d], c)
             own_state[d, c] = total
-            own_decay[d, c] = jnp.broadcast_to(decay, (8, CHUNK))
+            own_decay[d, c] = decay
             state_send[d, c, :state] = total.astype(BF16)
-            high, low = split(decay)
+            high, low = split(decay[0:1])
             state_send[d, c, state:] = jnp.where(
-                lax.broadcasted_iota(jnp.int32, (16, CHUNK), 0) == 0,
+                tail_row == 0,
                 high.astype(F32),
-                jnp.where(
-                    lax.broadcasted_iota(jnp.int32, (16, CHUNK), 0) == 1, low.astype(F32), 0.0
-                ),
+                jnp.where(tail_row == 1, low.astype(F32), 0.0),
             ).astype(BF16)
         remote(
             state_send.at[side, c],
@@ -248,7 +279,8 @@
                 direct = own if direct is None else jnp.where(mine, own, direct)
             head_out[:, columns] = result + direct * x_pair.astype(F32)
 
-    own_part(0, width // PAIR)
+    pairs = width // PAIR
+    own_part(0, pairs // 2)
 
     def chain_copy(c):
         return remote(
@@ -305,7 +337,16 @@
             chain_out[c] = (my_decay * entering + own_state[node_dir, c]).astype(BF16)
             chain_copy(c).start()
 
-    w_all[pl.ds(pl.multiple_of(my_dp * w_rows, w_rows), w_rows)] = w_ref[...]
+    own_part(pairs // 2, pairs)
+    for load in loads[4:]:
+        load.wait()
+    for c in range(chunks):
+        columns = slice(c * CHUNK, (c + 1) * CHUNK)
+        for d in range(2):
+            factor[d, :, columns] = widen(grows[d], c)
+        gate = gate_ref[0, :, columns].astype(F32)
+        silu[:, columns] = gate / (1.0 + jnp.exp(-gate))
+
     forwards = []
     for i, step in enumerate(range(2, n_dp, 2)):
         w_copies[i].wait_recv()
@@ -333,8 +374,7 @@
             + dot(c_f, incoming[0, c]) * factor[0, :, columns]
             + dot(c_b, incoming[1, c]) * factor[1, :, columns]
         )
-        gate = gate_ref[0, :, columns].astype(F32)
-        gated = mixed * (gate / (1.0 + jnp.exp(-gate)))
+        gated = mixed * silu[:, columns]
         spread_chunk = spread[:, columns]
         square = split(gated * gated)
         mean = (
@@ -464,9 +504,18 @@
             jax.ShapeDtypeStruct((1, rows, model), BF16),
             jax.ShapeDtypeStruct((1, queries, model), BF16),
         ),
-        in_specs=[smem, smem] + [vmem] * 8,
+        in_specs=[smem, smem] + [pl.BlockSpec(memory_space=pltpu.HBM)] * 8,
         out_specs=(vmem, vmem),
         scratch_shapes=[
+            pltpu.VMEM(ssm_input.shape, BF16),
+            pltpu.VMEM(gate_input.shape, BF16),
+            pltpu.VMEM(state_proj.shape, BF16),
+            pltpu.VMEM(step_raw.shape, F32),
+            pltpu.VMEM(decay_log.shape, F32),
+            pltpu.VMEM((1, width), F32),
+            pltpu.VMEM(latents.shape, BF16),
+            pltpu.VMEM((rows, width), F32),
+            dma((8,)),
             pltpu.VMEM((width, model), BF16),
             pltpu.VMEM((2, chunks, state, CHUNK), F32),
             pltpu.VMEM((2, chunks, 8, CHUNK), F32),

time: 62.9 us -> 65 us (1.033)
  Pallas kernels: 52.2 us -> 54.3 us
    pallas_call x1, Pallas kernels: 52.2 us -> 54.3 us  [body(): pl.pallas_call(functools.partial(kernel, n, n_dp), out_shape=(jax.ShapeDt...]
where the time goes in v2:
time: 65 us; the launch traced here: 64.4 us
  Pallas kernels  54.3 us (84%)
  local copies, waits for them, and re-layouts  8.81 us (14%)
  between operations  1.31 us (2%)
    pallas_call x1, Pallas kernels, body(): pl.pallas_call(functools.partial(kernel, n, n_dp), out_shape=(jax.ShapeDt...  54.3 us
    unnamed x20, local copies, waits for them, and re-layouts  8.81 us

profile of v2, /device:TPU:0, one launch (start us, length us, event | category | flops | bytes accessed | tf_op | source)
XLA Modules:
  0.0 64.4 jit_solution(12668785447490236418)
XLA Ops:
  1.3 0.0 copy-start.7
  1.3 0.0 copy-start.8
  1.3 0.7 %copy-done.7 = f32[2,16]{1,0:T(2,128)S(1)} copy-done((f32[2,16]{1,0:T(2,128)S(1)}, f32[2,16]{1,0:T(2,128)}, u32[]{:S(2)}) %copy-start.7) | copy-done | bytes 152
  2.0 0.0 copy-done.8
  2.0 0.0 copy-start
  2.0 1.0 %copy-done = bf16[1,256,1024]{2,1,0:T(8,128)(2,1)S(1)} copy-done((bf16[1,256,1024]{2,1,0:T(8,128)(2,1)S(1)}, bf16[1,256,1024]{2,1,0:T(8,128)(2,1)}, u32[]{:S(2)}) %copy-start) | copy-done | bytes 524312
  3.0 0.0 copy-start.1
  3.0 1.0 %copy-done.1 = bf16[1,256,1024]{2,1,0:T(8,128)(2,1)S(1)} copy-done((bf16[1,256,1024]{2,1,0:T(8,128)(2,1)S(1)}, bf16[1,256,1024]{2,1,0:T(8,128)(2,1)}, u32[]{:S(2)}) %copy-start.1) | copy-done | bytes 524312
  4.0 0.0 copy-start.2
  4.0 1.0 %copy-done.2 = bf16[256,1024]{1,0:T(8,128)(2,1)S(1)} copy-done((bf16[256,1024]{1,0:T(8,128)(2,1)S(1)}, bf16[256,1024]{1,0:T(8,128)(2,1)}, u32[]{:S(2)}) %copy-start.2) | copy-done | bytes 524312
  5.1 0.0 copy-start.3
  5.1 1.0 %copy-done.3 = bf16[256,1024]{1,0:T(8,128)(2,1)S(1)} copy-done((bf16[256,1024]{1,0:T(8,128)(2,1)S(1)}, bf16[256,1024]{1,0:T(8,128)(2,1)}, u32[]{:S(2)}) %copy-start.3) | copy-done | bytes 524312
  6.1 0.0 copy-start.4
  6.1 0.9 %copy-done.4 = bf16[1,256,512]{2,1,0:T(8,128)(2,1)S(1)} copy-done((bf16[1,256,512]{2,1,0:T(8,128)(2,1)S(1)}, bf16[1,256,512]{2,1,0:T(8,128)(2,1)}, u32[]{:S(2)}) %copy-start.4) | copy-done | bytes 262168
  7.1 0.0 copy-start.5
  7.1 0.8 %copy-done.5 = f32[1,32,256]{2,1,0:T(8,128)S(1)} copy-done((f32[1,32,256]{2,1,0:T(8,128)S(1)}, f32[1,32,256]{2,1,0:T(8,128)}, u32[]{:S(2)}) %copy-start.5) | copy-done | bytes 32792
  7.8 0.0 copy-start.6
  7.8 0.7 %copy-done.6 = f32[1024]{0:T(1024)S(1)} copy-done((f32[1024]{0:T(1024)S(1)}, f32[1024]{0:T(1024)}, u32[]{:S(2)}) %copy-start.6) | copy-done | bytes 4120
  8.5 54.3 %shard_map.113 = (bf16[1,256,1024]{2,1,0:T(8,128)(2,1)S(1)}, bf16[1,256,1024]{2,1,0:T(8,128)(2,1)S(1)}) custom-call(s32[1]{0:T(128)S(6)} %copy.14.lengths, f32[16]{0:T(128)S(1)} %copy-done.8, bf16[1,256,1024]{2,1,0:T(8,128)(2,1)S(1)} %copy-done, bf16[1,256,1024]{2,1,0:T(8,128)(2,1)S(1)} %copy-done.1, bf16[1,256,512]{2,1,0:T(8,128)(2,1)S(1)} %copy-done.4, ...), custom_call_target="tpu_custom_call" | custom-call | tf_op jit(solution)/shard_map/pallas_call | solution.py:501
  62.8 0.8 %copy.15 = bf16[1,256,1024]{2,1,0:T(8,128)(2,1)} copy(bf16[1,256,1024]{2,1,0:T(8,128)(2,1)S(1)} %get-tuple-element.4) | data formatting | bytes 1048576
  63.6 0.8 %copy.16 = bf16[1,256,1024]{2,1,0:T(8,128)(2,1)} copy(bf16[1,256,1024]{2,1,0:T(8,128)(2,1)S(1)} %get-tuple-element.5) | data formatting | bytes 1048576
Async XLA Ops:
  1.3 0.7 %copy-start.7 = (f32[2,16]{1,0:T(2,128)S(1)}, f32[2,16]{1,0:T(2,128)}, u32[]{:S(2)}) copy-start(f32[2,16]{1,0:T(2,128)} %decay_hbm.1) | copy-start | bytes 388
  1.3 0.7 %copy-start.8 = (f32[16]{0:T(128)S(1)}, f32[16]{0:T(128)}, u32[]{:S(2)}) copy-start(f32[16]{0:T(128)} %skip.1) | copy-start | bytes 196
  2.0 1.0 %copy-start = (bf16[1,256,1024]{2,1,0:T(8,128)(2,1)S(1)}, bf16[1,256,1024]{2,1,0:T(8,128)(2,1)}, u32[]{:S(2)}) copy-start(bf16[1,256,1024]{2,1,0:T(8,128)(2,1)} %x_hbm.1) | copy-start | bytes 1572868
  3.0 1.0 %copy-start.1 = (bf16[1,256,1024]{2,1,0:T(8,128)(2,1)S(1)}, bf16[1,256,1024]{2,1,0:T(8,128)(2,1)}, u32[]{:S(2)}) copy-start(bf16[1,256,1024]{2,1,0:T(8,128)(2,1)} %gate_hbm.1) | copy-start | bytes 1572868
  4.0 1.0 %copy-start.2 = (bf16[256,1024]{1,0:T(8,128)(2,1)S(1)}, bf16[256,1024]{1,0:T(8,128)(2,1)}, u32[]{:S(2)}) copy-start(bf16[256,1024]{1,0:T(8,128)(2,1)} %w_ref.1) | copy-start | bytes 1572868
  5.1 1.0 %copy-start.3 = (bf16[256,1024]{1,0:T(8,128)(2,1)S(1)}, bf16[256,1024]{1,0:T(8,128)(2,1)}, u32[]{:S(2)}) copy-start(bf16[256,1024]{1,0:T(8,128)(2,1)} %latents_hbm.1) | copy-start | bytes 1572868
  6.1 0.9 %copy-start.4 = (bf16[1,256,512]{2,1,0:T(8,128)(2,1)S(1)}, bf16[1,256,512]{2,1,0:T(8,128)(2,1)}, u32[]{:S(2)}) copy-start(bf16[1,256,512]{2,1,0:T(8,128)(2,1)} %proj_hbm.1) | copy-start | bytes 786436
  7.1 0.8 %copy-start.5 = (f32[1,32,256]{2,1,0:T(8,128)S(1)}, f32[1,32,256]{2,1,0:T(8,128)}, u32[]{:S(2)}) copy-start(f32[1,32,256]{2,1,0:T(8,128)} %raw_hbm.1) | copy-start | bytes 98308
  7.8 0.7 %copy-start.6 = (f32[1024]{0:T(1024)S(1)}, f32[1024]{0:T(1024)}, u32[]{:S(2)}) copy-start(f32[1024]{0:T(1024)} %param.16) | copy-start | bytes 12292

commit v3 on v2

--- a/solution.py
+++ b/solution.py
@@ -64,9 +64,9 @@
     factor,
     normed,
     sum_send,
-    stat_send,
+    sum_pair,
+    sum_both,
     sum_recv,
-    stat_recv,
     pool,
     w_send_sem,
     w_fwd_sem,
@@ -83,6 +83,8 @@
     stat_recv_sem,
     pool_send_sem,
     pool_recv_sem,
+    hand_send_sem,
+    hand_recv_sem,
 ):
     rows, width = x_ref.shape[1], x_ref.shape[2]
     heads = decay_ref.shape[1]
@@ -134,11 +136,13 @@
         load.start()
 
     barrier = pltpu.get_barrier_semaphore()
-    for step in range(1, n):
+    for neighbour in [partner] + [
+        2 * lax.rem(place + step, places) + side for step in range(1, places)
+    ]:
         pl.semaphore_signal(
             barrier,
             inc=1,
-            device_id={"seq": lax.rem(me + step, n)},
+            device_id={"seq": neighbour},
             device_id_type=pl.DeviceIdType.MESH,
         )
     pl.semaphore_signal(
@@ -151,7 +155,7 @@
             device_id={"dp": lax.rem(my_dp + step, n_dp)},
             device_id_type=pl.DeviceIdType.MESH,
         )
-    pl.semaphore_wait(barrier, n - 1 + n_dp // 2)
+    pl.semaphore_wait(barrier, places + n_dp // 2)
 
     def w_slot(owner):
         return w_all.at[pl.ds(pl.multiple_of(owner * w_rows, w_rows), w_rows)]
@@ -391,77 +395,123 @@
         enc_ref[0, :, columns] = dot(normed[...], w_all[:, columns]).astype(BF16)
 
     encoded = enc_ref[0]
-    scores = dot(latents_ref[...], encoded, ((1,), (1,))) * (1.0 / math.sqrt(encoded.shape[1]))
+    model = encoded.shape[1]
+    queries = latents_ref.shape[0]
+    share = queries // n
+
+    def parts_of(values):
+        first = values.astype(BF16).astype(F32)
+        second = (values - first).astype(BF16).astype(F32)
+        third = (values - first - second).astype(BF16).astype(F32)
+        return first, second, third
+
+    def tail_of(top, weight):
+        at = lax.broadcasted_iota(jnp.int32, (top.shape[0], 128), 1)
+        tail = jnp.zeros((top.shape[0], 128), F32)
+        for k, part in enumerate(parts_of(top) + parts_of(weight)):
+            tail = jnp.where(at == k, part, tail)
+        return tail.astype(BF16)
+
+    def read_tail(tail):
+        tail = tail.astype(F32)
+        top = tail[:, 0:1] + tail[:, 1:2] + tail[:, 2:3]
+        return top, tail[:, 3:4] + tail[:, 4:5] + tail[:, 5:6]
+
+    scores = dot(latents_ref[...], encoded, ((1,), (1,))) * (1.0 / math.sqrt(model))
     top = jnp.max(jnp.where(valid, scores, -1e30), axis=1, keepdims=True)
+    top = functools.reduce(jnp.add, parts_of(top))
     prob = jnp.where(valid, jnp.exp(scores - top), 0.0)
     weight_sum = jnp.sum(prob, axis=1, keepdims=True)
-    queries = latents_ref.shape[0]
-    share = queries // n
-    half = lax.broadcasted_iota(jnp.int32, (queries, 128), 1) < 64
-    stat_send[...] = jnp.where(half, top, weight_sum).reshape(n, share, 128)
+    tail = tail_of(top, weight_sum).astype(F32).reshape(places, 2, share, 128)
+    for s in range(2):
+        sum_send[s, :, :, model:] = tail[:, s].astype(BF16)
     prob_low = prob.astype(BF16)
-    for c in range(encoded.shape[1] // CHUNK):
+    for c in range(model // CHUNK):
         columns = slice(c * CHUNK, (c + 1) * CHUNK)
-        part = dot(prob_low, encoded[:, columns])
-        sum_send[:, :, columns] = part.reshape(n, share, CHUNK).astype(BF16)
-
-    sum_copies, stat_copies = [], []
-    for step in range(1, n):
-        target = lax.rem(me + step, n)
-        stat_copies.append(
-            remote(
-                stat_send.at[target],
-                stat_recv.at[step],
-                stat_send_sem.at[step],
-                stat_recv_sem.at[step],
-                seq=target,
-            )
-        )
-        sum_copies.append(
-            remote(
-                sum_send.at[target],
+        part = dot(prob_low, encoded[:, columns]).reshape(places, 2, share, CHUNK)
+        for s in range(2):
+            sum_send[s, :, :, columns] = part[:, s].astype(BF16)
+
+    def merge(messages):
+        stats = [read_tail(message[:, model:]) for message in messages]
+        best = functools.reduce(jnp.maximum, [t for t, _ in stats])
+        scales = [jnp.exp(t - best) for t, _ in stats]
+        weight = functools.reduce(jnp.add, [w * e for (_, w), e in zip(stats, scales)])
+        return best, weight, scales
+
+    def added(messages, scales):
+        return functools.reduce(
+            jnp.add,
+            [message[:, :model].astype(F32) * e for message, e in zip(messages, scales)],
+        )
+
+    pair_copies = []
+    for step in list(range(1, places)) + [0]:
+        target = lax.rem(place + step, places)
+        copy = remote(
+            sum_send.at[1 - side, target],
+            sum_pair.at[step],
+            stat_send_sem.at[step],
+            stat_recv_sem.at[step],
+            seq=partner,
+        )
+        copy.start()
+        pair_copies.append(copy)
+    sum_copies = []
+    for i, step in enumerate(list(range(1, places)) + [0]):
+        target = lax.rem(place + step, places)
+        pair_copies[i].wait_recv()
+        messages = [sum_send[side, target], sum_pair[step]]
+        best, weight, scales = merge(messages)
+        sum_both[step, :, :model] = added(messages, scales).astype(BF16)
+        sum_both[step, :, model:] = tail_of(best, weight)
+        if step > 0:
+            copy = remote(
+                sum_both.at[step],
                 sum_recv.at[step],
                 sum_send_sem.at[step],
                 sum_recv_sem.at[step],
-                seq=target,
+                seq=2 * target + side,
             )
-        )
-    for copy in stat_copies:
-        copy.start()
+            copy.start()
+            sum_copies.append(copy)
     for copy in sum_copies:
-        copy.start()
-    stat_recv[0] = stat_send[me]
-    for copy in stat_copies:
         copy.wait_recv()
-    tops = [stat_recv[step][:, 0:1] for step in range(n)]
-    best = functools.reduce(jnp.maximum, tops)
-    scales = [jnp.exp(t - best) for t in tops]
-    whole = functools.reduce(
-        jnp.add, [stat_recv[step][:, 64:65] * scales[step] for step in range(n)]
-    )
-    inverse = 1.0 / whole
-    total = sum_send[me].astype(F32) * (scales[0] * inverse)
-    for step in range(1, n):
-        sum_copies[step - 1].wait_recv()
-        total = total + sum_recv[step].astype(F32) * (scales[step] * inverse)
-    pool[me] = total.astype(BF16)
+    messages = [sum_both[0]] + [sum_recv[step] for step in range(1, places)]
+    best, weight, scales = merge(messages)
+    inverse = 1.0 / weight
+    pool[place, side] = added(messages, [e * inverse for e in scales]).astype(BF16)
+
+    def hand_on(step):
+        slot = pool.at[lax.rem(place + places - step, places), side]
+        return remote(
+            slot, slot, hand_send_sem.at[step], hand_recv_sem.at[step], seq=partner
+        )
+
     pool_copies = []
-    for step in range(1, n):
-        target = lax.rem(me + step, n)
+    for step in range(1, places):
+        target = lax.rem(place + step, places)
         copy = remote(
-            pool.at[me],
-            pool.at[me],
+            pool.at[place, side],
+            pool.at[place, side],
             pool_send_sem.at[step],
             pool_recv_sem.at[step],
-            seq=target,
+            seq=2 * target + side,
         )
         copy.start()
         pool_copies.append(copy)
-    for copy in pool_copies:
+    hand_copies = [hand_on(0)]
+    hand_copies[0].start()
+    for step in range(1, places):
+        pool_copies[step - 1].wait_recv()
+        copy = hand_on(step)
+        copy.start()
+        hand_copies.append(copy)
+    for copy in hand_copies:
         copy.wait_recv()
-    pooled_ref[0] = pool[...].reshape(queries, pool.shape[2])
-
-    for copy in w_copies + forwards + sum_copies + stat_copies + pool_copies:
+    pooled_ref[0] = pool[...].reshape(queries, model)
+
+    for copy in w_copies + forwards + pair_copies + sum_copies + pool_copies + hand_copies:
         copy.wait_send()
     for c in range(chunks):
         pair_copy(c).wait_send()
@@ -528,11 +578,11 @@
             pltpu.VMEM((rows, width), F32),
             pltpu.VMEM((2, rows, width), F32),
             pltpu.VMEM((rows, width), BF16),
-            pltpu.VMEM((n, share, model), BF16),
-            pltpu.VMEM((n, share, 128), F32),
-            pltpu.VMEM((n, share, model), BF16),
-            pltpu.VMEM((n, share, 128), F32),
-            pltpu.VMEM((n, share, model), BF16),
+            pltpu.VMEM((2, n // 2, share, model + 128), BF16),
+            pltpu.VMEM((n // 2, share, model + 128), BF16),
+            pltpu.VMEM((n // 2, share, model + 128), BF16),
+            pltpu.VMEM((n // 2, share, model + 128), BF16),
+            pltpu.VMEM((n // 2, 2, share, model), BF16),
             dma((n_dp,)),
             dma((n_dp,)),
             dma((n_dp,)),
@@ -542,12 +592,14 @@
             dma((chunks,)),
             dma((chunks,)),
             dma((chunks,)),
-            dma((n,)),
-            dma((n,)),
-            dma((n,)),
-            dma((n,)),
-            dma((n,)),
-            dma((n,)),
+            dma((n // 2,)),
+            dma((n // 2,)),
+            dma((n // 2,)),
+            dma((n // 2,)),
+            dma((n // 2,)),
+            dma((n // 2,)),
+            dma((n // 2,)),
+            dma((n // 2,)),
         ],
         compiler_params=pltpu.CompilerParams(
             collective_id=0, has_side_effects=True, vmem_limit_bytes=48 * 1024 * 1024

time: 65 us -> 63.9 us (0.983)
  Pallas kernels: 54.3 us -> 53.3 us
    pallas_call x1, Pallas kernels: 54.3 us -> 53.3 us  [body(): pl.pallas_call(functools.partial(kernel, n, n_dp), out_shape=(jax.ShapeDt...]
where the time goes in v3:
time: 63.9 us; the launch traced here: 63.5 us
  Pallas kernels  53.3 us (83%)
  local copies, waits for them, and re-layouts  8.81 us (14%)
  between operations  1.31 us (2%)
    pallas_call x1, Pallas kernels, body(): pl.pallas_call(functools.partial(kernel, n, n_dp), out_shape=(jax.ShapeDt...  53.3 us
    unnamed x20, local copies, waits for them, and re-layouts  8.81 us

profile of v3, /device:TPU:0, one launch (start us, length us, event | category | flops | bytes accessed | tf_op | source)
XLA Modules:
  0.0 63.5 jit_solution(5624878037167413345)
XLA Ops:
  1.3 0.0 copy-start.7
  1.3 0.0 copy-start.8
  1.3 0.7 %copy-done.7 = f32[2,16]{1,0:T(2,128)S(1)} copy-done((f32[2,16]{1,0:T(2,128)S(1)}, f32[2,16]{1,0:T(2,128)}, u32[]{:S(2)}) %copy-start.7) | copy-done | bytes 152
  2.0 0.0 copy-done.8
  2.0 0.0 copy-start
  2.0 1.0 %copy-done = bf16[1,256,1024]{2,1,0:T(8,128)(2,1)S(1)} copy-done((bf16[1,256,1024]{2,1,0:T(8,128)(2,1)S(1)}, bf16[1,256,1024]{2,1,0:T(8,128)(2,1)}, u32[]{:S(2)}) %copy-start) | copy-done | bytes 524312
  3.0 0.0 copy-start.1
  3.0 1.0 %copy-done.1 = bf16[1,256,1024]{2,1,0:T(8,128)(2,1)S(1)} copy-done((bf16[1,256,1024]{2,1,0:T(8,128)(2,1)S(1)}, bf16[1,256,1024]{2,1,0:T(8,128)(2,1)}, u32[]{:S(2)}) %copy-start.1) | copy-done | bytes 524312
  4.0 0.0 copy-start.2
  4.0 1.0 %copy-done.2 = bf16[256,1024]{1,0:T(8,128)(2,1)S(1)} copy-done((bf16[256,1024]{1,0:T(8,128)(2,1)S(1)}, bf16[256,1024]{1,0:T(8,128)(2,1)}, u32[]{:S(2)}) %copy-start.2) | copy-done | bytes 524312
  5.1 0.0 copy-start.3
  5.1 1.0 %copy-done.3 = bf16[256,1024]{1,0:T(8,128)(2,1)S(1)} copy-done((bf16[256,1024]{1,0:T(8,128)(2,1)S(1)}, bf16[256,1024]{1,0:T(8,128)(2,1)}, u32[]{:S(2)}) %copy-start.3) | copy-done | bytes 524312
  6.1 0.0 copy-start.4
  6.1 0.9 %copy-done.4 = bf16[1,256,512]{2,1,0:T(8,128)(2,1)S(1)} copy-done((bf16[1,256,512]{2,1,0:T(8,128)(2,1)S(1)}, bf16[1,256,512]{2,1,0:T(8,128)(2,1)}, u32[]{:S(2)}) %copy-start.4) | copy-done | bytes 262168
  7.1 0.0 copy-start.5
  7.1 0.8 %copy-done.5 = f32[1,32,256]{2,1,0:T(8,128)S(1)} copy-done((f32[1,32,256]{2,1,0:T(8,128)S(1)}, f32[1,32,256]{2,1,0:T(8,128)}, u32[]{:S(2)}) %copy-start.5) | copy-done | bytes 32792
  7.8 0.0 copy-start.6
  7.8 0.7 %copy-done.6 = f32[1024]{0:T(1024)S(1)} copy-done((f32[1024]{0:T(1024)S(1)}, f32[1024]{0:T(1024)}, u32[]{:S(2)}) %copy-start.6) | copy-done | bytes 4120
  8.5 53.3 %shard_map.113 = (bf16[1,256,1024]{2,1,0:T(8,128)(2,1)S(1)}, bf16[1,256,1024]{2,1,0:T(8,128)(2,1)S(1)}) custom-call(s32[1]{0:T(128)S(6)} %copy.14.lengths, f32[16]{0:T(128)S(1)} %copy-done.8, bf16[1,256,1024]{2,1,0:T(8,128)(2,1)S(1)} %copy-done, bf16[1,256,1024]{2,1,0:T(8,128)(2,1)S(1)} %copy-done.1, bf16[1,256,512]{2,1,0:T(8,128)(2,1)S(1)} %copy-done.4, ...), custom_call_target="tpu_custom_call" | custom-call | tf_op jit(solution)/shard_map/pallas_call | solution.py:551
  61.9 0.8 %copy.15 = bf16[1,256,1024]{2,1,0:T(8,128)(2,1)} copy(bf16[1,256,1024]{2,1,0:T(8,128)(2,1)S(1)} %get-tuple-element.4) | data formatting | bytes 1048576
  62.7 0.8 %copy.16 = bf16[1,256,1024]{2,1,0:T(8,128)(2,1)} copy(bf16[1,256,1024]{2,1,0:T(8,128)(2,1)S(1)} %get-tuple-element.5) | data formatting | bytes 1048576
Async XLA Ops:
  1.3 0.7 %copy-start.7 = (f32[2,16]{1,0:T(2,128)S(1)}, f32[2,16]{1,0:T(2,128)}, u32[]{:S(2)}) copy-start(f32[2,16]{1,0:T(2,128)} %decay_hbm.1) | copy-start | bytes 388
  1.3 0.7 %copy-start.8 = (f32[16]{0:T(128)S(1)}, f32[16]{0:T(128)}, u32[]{:S(2)}) copy-start(f32[16]{0:T(128)} %skip.1) | copy-start | bytes 196
  2.0 1.0 %copy-start = (bf16[1,256,1024]{2,1,0:T(8,128)(2,1)S(1)}, bf16[1,256,1024]{2,1,0:T(8,128)(2,1)}, u32[]{:S(2)}) copy-start(bf16[1,256,1024]{2,1,0:T(8,128)(2,1)} %x_hbm.1) | copy-start | bytes 1572868
  3.0 1.0 %copy-start.1 = (bf16[1,256,1024]{2,1,0:T(8,128)(2,1)S(1)}, bf16[1,256,1024]{2,1,0:T(8,128)(2,1)}, u32[]{:S(2)}) copy-start(bf16[1,256,1024]{2,1,0:T(8,128)(2,1)} %gate_hbm.1) | copy-start | bytes 1572868
  4.0 1.0 %copy-start.2 = (bf16[256,1024]{1,0:T(8,128)(2,1)S(1)}, bf16[256,1024]{1,0:T(8,128)(2,1)}, u32[]{:S(2)}) copy-start(bf16[256,1024]{1,0:T(8,128)(2,1)} %w_ref.1) | copy-start | bytes 1572868
  5.1 1.0 %copy-start.3 = (bf16[256,1024]{1,0:T(8,128)(2,1)S(1)}, bf16[256,1024]{1,0:T(8,128)(2,1)}, u32[]{:S(2)}) copy-start(bf16[256,1024]{1,0:T(8,128)(2,1)} %latents_hbm.1) | copy-start | bytes 1572868
  6.1 0.9 %copy-start.4 = (bf16[1,256,512]{2,1,0:T(8,128)(2,1)S(1)}, bf16[1,256,512]{2,1,0:T(8,128)(2,1)}, u32[]{:S(2)}) copy-start(bf16[1,256,512]{2,1,0:T(8,128)(2,1)} %proj_hbm.1) | copy-start | bytes 786436
  7.1 0.8 %copy-start.5 = (f32[1,32,256]{2,1,0:T(8,128)S(1)}, f32[1,32,256]{2,1,0:T(8,128)}, u32[]{:S(2)}) copy-start(f32[1,32,256]{2,1,0:T(8,128)} %raw_hbm.1) | copy-start | bytes 98308
  7.8 0.7 %copy-start.6 = (f32[1024]{0:T(1024)S(1)}, f32[1024]{0:T(1024)}, u32[]{:S(2)}) copy-start(f32[1024]{0:T(1024)} %param.16) | copy-start | bytes 12292

commit v4 on v3

--- a/solution.py
+++ b/solution.py
@@ -10,6 +10,7 @@
 
 CHUNK = 256
 PAIR = 128
+VMEM_BYTES = 63 * 1024 * 1024 + 512 * 1024
 F32 = jnp.float32
 BF16 = jnp.bfloat16
 
@@ -284,7 +285,8 @@
             head_out[:, columns] = result + direct * x_pair.astype(F32)
 
     pairs = width // PAIR
-    own_part(0, pairs // 2)
+    pl.when(along >= 1)(lambda: own_part(0, pairs // 2))
+    pl.when(along >= 2)(lambda: own_part(pairs // 2, pairs))
 
     def chain_copy(c):
         return remote(
@@ -341,7 +343,8 @@
             chain_out[c] = (my_decay * entering + own_state[node_dir, c]).astype(BF16)
             chain_copy(c).start()
 
-    own_part(pairs // 2, pairs)
+    pl.when(along < 1)(lambda: own_part(0, pairs // 2))
+    pl.when(along < 2)(lambda: own_part(pairs // 2, pairs))
     for load in loads[4:]:
         load.wait()
     for c in range(chunks):
@@ -602,7 +605,7 @@
             dma((n // 2,)),
         ],
         compiler_params=pltpu.CompilerParams(
-            collective_id=0, has_side_effects=True, vmem_limit_bytes=48 * 1024 * 1024
+            collective_id=0, has_side_effects=True, vmem_limit_bytes=VMEM_BYTES
         ),
     )(
         lengths,

time: 63.9 us -> 57.3 us (0.90)
  local copies, waits for them, and re-layouts: 8.81 us -> 2.72 us
    unnamed x20 -> x4, local copies, waits for them, and re-layouts: 8.81 us -> 2.72 us
where the time goes in v4:
time: 57.3 us; the launch traced here: 57.1 us
  Pallas kernels  53.1 us (93%)
  local copies, waits for them, and re-layouts  2.72 us (5%)
  between operations  1.3 us (2%)
    pallas_call x1, Pallas kernels, body(): pl.pallas_call(functools.partial(kernel, n, n_dp), out_shape=(jax.ShapeDt...  53.1 us
    unnamed x4, local copies, waits for them, and re-layouts  2.72 us

profile of v4, /device:TPU:0, one launch (start us, length us, event | category | flops | bytes accessed | tf_op | source)
XLA Modules:
  0.0 57.1 jit_solution(4095694459631626643)
XLA Ops:
  1.3 53.1 %shard_map.113 = (bf16[1,256,1024]{2,1,0:T(8,128)(2,1)}, bf16[1,256,1024]{2,1,0:T(8,128)(2,1)}) custom-call(s32[1]{0:T(128)S(6)} %copy.14.lengths, f32[16]{0:T(128)} %skip.1, bf16[1,256,1024]{2,1,0:T(8,128)(2,1)} %x_hbm.1, bf16[1,256,1024]{2,1,0:T(8,128)(2,1)} %gate_hbm.1, bf16[1,256,512]{2,1,0:T(8,128)(2,1)} %proj_hbm.1, f32[1,32,256]{2,1,0:T(8,128)} %raw_hbm.1, ...), custom_call_target="tpu_custom_call" | custom-call | tf_op jit(solution)/shard_map/pallas_call | solution.py:554
  54.4 0.0 copy-start
  54.4 1.9 %copy.15 = bf16[1,256,1024]{2,1,0:T(8,128)(2,1)} copy(bf16[1,256,1024]{2,1,0:T(8,128)(2,1)} %get-tuple-element.4) | data formatting | bytes 1048576
  56.3 0.0 copy-done
  56.3 0.8 %copy.16 = bf16[1,256,1024]{2,1,0:T(8,128)(2,1)} copy(bf16[1,256,1024]{2,1,0:T(8,128)(2,1)S(1)} %copy-done) | data formatting | bytes 1048576
Async XLA Ops:
  54.4 1.9 %copy-start = (bf16[1,256,1024]{2,1,0:T(8,128)(2,1)S(1)}, bf16[1,256,1024]{2,1,0:T(8,128)(2,1)}, u32[]{:S(2)}) copy-start(bf16[1,256,1024]{2,1,0:T(8,128)(2,1)} %get-tuple-element.5) | copy-start | bytes 1572868

commit v5 on v4

--- a/solution.py
+++ b/solution.py
@@ -284,9 +284,20 @@
                 direct = own if direct is None else jnp.where(mine, own, direct)
             head_out[:, columns] = result + direct * x_pair.astype(F32)
 
+    def prepare():
+        for load in loads[4:7]:
+            load.wait()
+        for c in range(chunks):
+            columns = slice(c * CHUNK, (c + 1) * CHUNK)
+            for d in range(2):
+                factor[d, :, columns] = widen(grows[d], c)
+            gate = gate_ref[0, :, columns].astype(F32)
+            silu[:, columns] = gate / (1.0 + jnp.exp(-gate))
+
     pairs = width // PAIR
     pl.when(along >= 1)(lambda: own_part(0, pairs // 2))
     pl.when(along >= 2)(lambda: own_part(pairs // 2, pairs))
+    pl.when(along >= 2)(prepare)
 
     def chain_copy(c):
         return remote(
@@ -345,15 +356,9 @@
 
     pl.when(along < 1)(lambda: own_part(0, pairs // 2))
     pl.when(along < 2)(lambda: own_part(pairs // 2, pairs))
-    for load in loads[4:]:
-        load.wait()
-    for c in range(chunks):
-        columns = slice(c * CHUNK, (c + 1) * CHUNK)
-        for d in range(2):
-            factor[d, :, columns] = widen(grows[d], c)
-        gate = gate_ref[0, :, columns].astype(F32)
-        silu[:, columns] = gate / (1.0 + jnp.exp(-gate))
-
+    pl.when(along < 2)(prepare)
+
+    loads[7].wait()
     forwards = []
     for i, step in enumerate(range(2, n_dp, 2)):
         w_copies[i].wait_recv()

time: 57.3 us -> 56.5 us (0.986)
  Pallas kernels: 53.1 us -> 52.4 us
    pallas_call x1, Pallas kernels: 53.1 us -> 52.4 us  [body(): pl.pallas_call(functools.partial(kernel, n, n_dp), out_shape=(jax.ShapeDt...]
where the time goes in v5:
time: 56.5 us; the launch traced here: 56.4 us
  Pallas kernels  52.4 us (93%)
  local copies, waits for them, and re-layouts  2.72 us (5%)
  between operations  1.3 us (2%)
    pallas_call x1, Pallas kernels, body(): pl.pallas_call(functools.partial(kernel, n, n_dp), out_shape=(jax.ShapeDt...  52.4 us
    unnamed x4, local copies, waits for them, and re-layouts  2.72 us

profile of v5, /device:TPU:0, one launch (start us, length us, event | category | flops | bytes accessed | tf_op | source)
XLA Modules:
  0.0 56.4 jit_solution(10970960123705539846)
XLA Ops:
  1.3 52.4 %shard_map.113 = (bf16[1,256,1024]{2,1,0:T(8,128)(2,1)}, bf16[1,256,1024]{2,1,0:T(8,128)(2,1)}) custom-call(s32[1]{0:T(128)S(6)} %copy.14.lengths, f32[16]{0:T(128)} %skip.1, bf16[1,256,1024]{2,1,0:T(8,128)(2,1)} %x_hbm.1, bf16[1,256,1024]{2,1,0:T(8,128)(2,1)} %gate_hbm.1, bf16[1,256,512]{2,1,0:T(8,128)(2,1)} %proj_hbm.1, f32[1,32,256]{2,1,0:T(8,128)} %raw_hbm.1, ...), custom_call_target="tpu_custom_call" | custom-call | tf_op jit(solution)/shard_map/pallas_call | solution.py:559
  53.6 0.0 copy-start
  53.7 1.9 %copy.15 = bf16[1,256,1024]{2,1,0:T(8,128)(2,1)} copy(bf16[1,256,1024]{2,1,0:T(8,128)(2,1)} %get-tuple-element.4) | data formatting | bytes 1048576
  55.6 0.0 copy-done
  55.6 0.8 %copy.16 = bf16[1,256,1024]{2,1,0:T(8,128)(2,1)} copy(bf16[1,256,1024]{2,1,0:T(8,128)(2,1)S(1)} %copy-done) | data formatting | bytes 1048576
Async XLA Ops:
  53.6 1.9 %copy-start = (bf16[1,256,1024]{2,1,0:T(8,128)(2,1)S(1)}, bf16[1,256,1024]{2,1,0:T(8,128)(2,1)}, u32[]{:S(2)}) copy-start(bf16[1,256,1024]{2,1,0:T(8,128)(2,1)} %get-tuple-element.5) | copy-start | bytes 1572868
